TPU v7x, 32 devices: a whole 2x2x4 slice. The times are simulated.
32 devices in a mesh: sweep: 2 (over x), row: 16 (over z, y, core).
Axes of the slice: x: 2, y: 2, z: 4, core: 2. Of those that a mesh axis runs over, the one named last changes fastest.
Arguments:
- alphas: float32 [4], P('sweep'), parts along dimension 0, may hold values from 0.75 to 0.95
- base_scores: float32 [172, 16384], P(None, 'row'), may hold values from 0 to 1
- tile_values: bfloat16 [2560, 128, 128], P('row')
- tile_rows: int32 [2560], P('row'), may hold values from 0 to 7
- tile_cols: int32 [2560], P('row'), may hold values from 0 to 8
- send_rows: int32 [16, 4, 32], P('row'), may hold values from 0 to 1023
- send_count: int32 [16, 4], P('row'), may hold values from 0 to 32, as said below
- train_nodes: int32 [1024], P('row'), may hold values from 0 to 1023, as said below
- train_labels: int32 [1024], P('row'), may hold values from 0 to 171
Outputs:
- smoothed: float32 [344, 16384], P('sweep', 'row'), parts along dimension 0
There are 2 independent parts, one for each index of `sweep`. A program takes and returns all parts, laid end to end along the dimension named above; an argument that names none is the same for every part. Nothing has to cross between parts.
Inputs may be any that keep to these rules, and one draw needn't show every extreme that they name: `send_count`: zero where the receiving partition index lies outside the axis; in every draw one partition receives 32 live entries from each of its neighbours. `train_nodes`: distinct within each partition's block of 64 entries.
All inputs are finite; a program needn't handle non-finite values.
Results may differ from a plain program's by a relative error of at most 0.00093.
Values may be sent and summed in bfloat16 or wider, within the bound.
A program may use at most 128 MiB of HBM per device.

v0:
```python
import functools

import jax
import jax.numpy as jnp
from jax import lax
from jax.experimental import pallas as pl
from jax.experimental.pallas import tpu as pltpu
from jax.sharding import PartitionSpec as P

CHUNKS = 8
MESH = pl.DeviceIdType.MESH
BF = jnp.bfloat16
F32 = jnp.float32


def dot(a, b):
    return jnp.dot(a, b, preferred_element_type=F32)


def dot_nt(a, b, precision=None):
    return lax.dot_general(a, b, (((1,), (1,)), ((), ())), precision=precision, preferred_element_type=F32)


def dot_tn(a, b):
    return lax.dot_general(a, b, (((0,), (0,)), ((), ())), preferred_element_type=F32)


def split(x):
    high = x.astype(BF)
    return high, (x - high.astype(F32)).astype(BF)


def dense_body(rows, cols, tiles, high, low, held, acc, sems):
    count, tile, _ = tiles.shape
    col_blocks, row_blocks = acc.shape[:2]
    step = count // CHUNKS
    copies = []
    for chunk in range(CHUNKS):
        part = pl.ds(chunk * step, step)
        copies.append(pltpu.make_async_copy(tiles.at[part], held.at[part], sems.at[chunk]))
        copies[-1].start()
    acc[...] = jnp.zeros_like(acc)
    for chunk in range(CHUNKS):
        copies[chunk].wait()

        def add(t, _):
            at = (cols[t], rows[t])
            acc[at] += held[t].astype(F32)
            return 0

        lax.fori_loop(chunk * step, (chunk + 1) * step, add, 0, unroll=4)
    for c in range(col_blocks):
        for r in range(row_blocks):
            high_part, low_part = split(acc[c, r])
            high[c * tile : (c + 1) * tile, r * tile : (r + 1) * tile] = high_part
            low[c * tile : (c + 1) * tile, r * tile : (r + 1) * tile] = low_part


def dense(tile_rows, tile_cols, tile_values, nodes, halo):
    count, tile, _ = tile_values.shape
    shape = jax.ShapeDtypeStruct((nodes + halo, nodes), BF)
    return pl.pallas_call(
        dense_body,
        out_shape=(shape, shape),
        in_specs=[
            pl.BlockSpec(memory_space=pltpu.SMEM),
            pl.BlockSpec(memory_space=pltpu.SMEM),
            pl.BlockSpec(memory_space=pl.ANY),
        ],
        out_specs=(pl.BlockSpec(memory_space=pltpu.VMEM),) * 2,
        scratch_shapes=[
            pltpu.VMEM((count, tile, tile), BF),
            pltpu.VMEM(((nodes + halo) // tile, nodes // tile, tile, tile), F32),
            pltpu.SemaphoreType.DMA((CHUNKS,)),
        ],
        compiler_params=pltpu.CompilerParams(vmem_limit_bytes=40 << 20),
        name="dense",
    )(tile_rows, tile_cols, tile_values)


def spread_body(
    n, alphas, counts, base, send_rows, nodes, labels, high_in, low_in, out,
    high, low, pick, start, fixed, truth, sent0, sent1, sent2, sent3, got0, got1, got2, got3,
    part, parts, send_sems, recv_sems, part_send, part_recv, load_sems,
):
    channels, local = base.shape
    slots, size = send_rows.shape[1:]
    reach = slots // 2
    offsets = [value for value in range(-reach, reach + 1) if value != 0]
    me = lax.axis_index("row")
    sent, got = (sent0, sent1, sent2, sent3), (got0, got1, got2, got3)

    barrier = pltpu.get_barrier_semaphore()

    def greet(k, _):
        pl.semaphore_signal(barrier, inc=1, device_id={"row": lax.rem(me + k, n)}, device_id_type=MESH)
        return 0

    lax.fori_loop(1, n, greet, 0)
    loads = [pltpu.make_async_copy(high_in, high, load_sems.at[0]), pltpu.make_async_copy(low_in, low, load_sems.at[1])]
    for load in loads:
        load.start()

    def inside(offset):
        return (me + offset >= 0) & (me + offset < n)

    for slot, offset in enumerate(offsets):

        @pl.when(jnp.logical_not(inside(offset)))
        def _():
            for buffer in got:
                buffer[slot] = jnp.zeros(buffer.shape[1:], BF)

    def copy(turn, k):
        return pltpu.make_async_remote_copy(
            src_ref=sent[turn].at[k],
            dst_ref=got[turn].at[slots - 1 - k],
            send_sem=send_sems.at[turn, k],
            recv_sem=recv_sems.at[turn, slots - 1 - k],
            device_id={"row": me + offsets[k]},
            device_id_type=MESH,
        )

    def send(turn, planes):
        picked = [dot_nt(pick[...], plane).astype(BF) for plane in planes]
        for k in range(slots):
            for at, plane in enumerate(picked):
                sent[turn][k, at * size : (at + 1) * size, :] = plane[k * size : (k + 1) * size, :]

    def launch(turn):
        for k, offset in enumerate(offsets):

            @pl.when(inside(offset))
            def _():
                copy(turn, k).start()

    def receive(turn):
        for slot, offset in enumerate(offsets):

            @pl.when(inside(offset))
            def _():
                copy(turn, slots - 1 - slot).wait_recv()

        planes = got[turn].shape[1] // size
        return [
            jnp.concatenate([got[turn][slot, at * size : (at + 1) * size, :] for slot in range(slots)], axis=0)
            for at in range(planes)
        ]

    def local_product(values):
        return dot(values, high[:local, :]) + dot(values, low[:local, :])

    def halo_product(values):
        return dot_tn(values, high[local:, :]) + dot_tn(values, low[local:, :])

    eye = jnp.where(
        lax.broadcasted_iota(jnp.int32, (size, size), 0) == lax.broadcasted_iota(jnp.int32, (size, size), 1), 1.0, 0.0
    ).astype(F32)
    wanted = dot_nt(eye, send_rows[0].astype(F32), precision=lax.Precision.HIGHEST).astype(jnp.int32)
    column = lax.broadcasted_iota(jnp.int32, (size, local), 1)
    place = lax.broadcasted_iota(jnp.int32, (size, local), 0)
    for k in range(slots):
        live = (column == wanted[:, k : k + 1]) & (place < counts[0, k])
        pick[k * size : (k + 1) * size, :] = jnp.where(live, 1.0, 0.0).astype(BF)

    count = nodes.shape[1]
    placed = jnp.where(lax.broadcasted_iota(jnp.int32, (local, count), 0) == nodes[...], 1.0, 0.0).astype(BF)
    onehot = jnp.where(lax.broadcasted_iota(jnp.int32, (channels, count), 0) == labels[...], 1.0, 0.0).astype(BF)
    truth[...] = dot_nt(onehot, placed)
    labelled = dot_nt(jnp.ones((8, count), BF), placed)[0:1, :]
    free = 1.0 - labelled
    start[...] = labelled * (truth[...] - base[...])
    fixed[...] = truth[...] + free * base[...]
    values = start[...].astype(BF)
    fixed_high, fixed_low = split(fixed[...])
    send(0, [values, fixed_high, fixed_low])
    pl.semaphore_wait(barrier, n - 1)
    launch(0)

    def folded(x):
        row = jnp.sum(x, axis=0, keepdims=True)
        return sum(row[:, at : at + 128] for at in range(0, local, 128))

    part[...] = jnp.zeros_like(part)
    part[0:1, :] = folded(jnp.abs(start[...]))

    weight = alphas[0]
    for load in loads:
        load.wait()
    total = local_product(values)
    total = total + halo_product(receive(0)[0])
    errors = (1.0 - weight) * start[...] + weight * total
    values = errors.astype(BF)
    send(1, [values])
    launch(1)
    total = local_product(values)
    total = total + halo_product(receive(1)[0])
    errors = (1.0 - weight) * start[...] + weight * total
    part[1:2, :] = folded(labelled * jnp.abs(errors))

    def part_copy(k):
        return pltpu.make_async_remote_copy(
            src_ref=part,
            dst_ref=parts.at[k - 1],
            send_sem=part_send.at[k - 1],
            recv_sem=part_recv.at[k - 1],
            device_id={"row": lax.rem(me + k, n)},
            device_id_type=MESH,
        )

    def part_start(k, _):
        part_copy(k).start()
        return 0

    lax.fori_loop(1, n, part_start, 0)
    moving = free * errors
    moving_high, moving_low = split(moving)
    send(2, [moving_high, moving_low])
    launch(2)

    def part_wait(k, _):
        part_copy(k).wait_recv()
        return 0

    lax.fori_loop(1, n, part_wait, 0)
    sums = part[...] + jnp.sum(parts[...], axis=0)
    entries = n * count * channels
    mass = jnp.sum(sums[0:1, :], axis=1, keepdims=True) / entries
    spread = jnp.sum(sums[1:2, :], axis=1, keepdims=True) / entries
    scale = mass / (spread + 1e-06)
    anchored = fixed[...] + scale * moving
    start[...] = anchored
    values = anchored.astype(BF)
    weight = alphas[1]
    total = local_product(values)
    fixed_high, fixed_low = [
        jnp.concatenate([got0[slot, at * size : (at + 1) * size, :] for slot in range(slots)], axis=0).astype(F32)
        for at in (1, 2)
    ]
    moving_high, moving_low = [plane.astype(F32) for plane in receive(2)]
    halo = (fixed_high + fixed_low) + scale * (moving_high + moving_low)
    total = total + halo_product(halo.astype(BF))
    smoothed = truth[...] + free * ((1.0 - weight) * start[...] + weight * total)
    values = smoothed.astype(BF)
    send(3, [values])
    launch(3)
    total = local_product(values)
    total = total + halo_product(receive(3)[0])
    out[...] = truth[...] + free * ((1.0 - weight) * start[...] + weight * total)

    for turn in range(4):
        for k, offset in enumerate(offsets):

            @pl.when(inside(offset))
            def _():
                copy(turn, k).wait_send()

    def part_end(k, _):
        part_copy(k).wait_send()
        return 0

    lax.fori_loop(1, n, part_end, 0)


def shards(
    alphas, base_scores, tile_values, tile_rows, tile_cols, send_rows, send_count, train_nodes, train_labels
):
    n = lax.axis_size("row")
    channels, local = base_scores.shape
    slots, size = send_rows.shape[1:]
    halo = slots * size
    high, low = dense(tile_rows, tile_cols, tile_values, local, halo)
    vmem = pl.BlockSpec(memory_space=pltpu.VMEM)
    smem = pl.BlockSpec(memory_space=pltpu.SMEM)
    hbm = pl.BlockSpec(memory_space=pl.ANY)
    whole = pltpu.VMEM((channels, local), F32)
    planes = (3, 1, 2, 1)
    boundary = [pltpu.VMEM((slots, size * p, channels), BF) for p in planes]
    return pl.pallas_call(
        functools.partial(spread_body, n),
        out_shape=jax.ShapeDtypeStruct((channels, local), F32),
        in_specs=[smem, smem, vmem, vmem, vmem, vmem, hbm, hbm],
        out_specs=vmem,
        scratch_shapes=[
            pltpu.VMEM(high.shape, BF),
            pltpu.VMEM(low.shape, BF),
            pltpu.VMEM((halo, local), BF),
            whole,
            whole,
            whole,
            *boundary,
            *boundary,
            pltpu.VMEM((8, 128), F32),
            pltpu.VMEM((n - 1, 8, 128), F32),
            pltpu.SemaphoreType.DMA((4, slots)),
            pltpu.SemaphoreType.DMA((4, slots)),
            pltpu.SemaphoreType.DMA((n - 1,)),
            pltpu.SemaphoreType.DMA((n - 1,)),
            pltpu.SemaphoreType.DMA((2,)),
        ],
        compiler_params=pltpu.CompilerParams(collective_id=0, has_side_effects=True, vmem_limit_bytes=40 << 20),
        name="spread",
    )(
        alphas, send_count, base_scores, send_rows,
        train_nodes.reshape(1, -1), train_labels.reshape(1, -1), high, low,
    )


def solution(mesh):
    return jax.shard_map(
        shards,
        mesh=mesh,
        in_specs=(
            P("sweep"), P(None, "row"), P("row", None, None), P("row"), P("row"),
            P("row", None, None), P("row", None), P("row"), P("row"),
        ),
        out_specs=P("sweep", "row"),
        check_vma=False,
    )
```

profile of v0, /device:TPU:0, one launch (start us, length us, event | category | flops | bytes accessed | tf_op | source)
XLA Modules:
  0.0 34.4 jit_solution(18131014514520279694)
XLA Ops:
  0.0 0.0 copy-start
  0.0 2.5 %copy-done = bf16[160,128,128]{2,1,0:T(8,128)(2,1)S(1)} copy-done((bf16[160,128,128]{2,1,0:T(8,128)(2,1)S(1)}, bf16[160,128,128]{2,1,0:T(8,128)(2,1)}, u32[]{:S(2)}) %copy-start) | copy-done | bytes 5242904
  2.5 0.0 copy-start.3
  2.5 0.7 %copy-done.3 = s32[160]{0:T(256)S(1)} copy-done((s32[160]{0:T(256)S(1)}, s32[160]{0:T(256)}, u32[]{:S(2)}) %copy-start.3) | copy-done | bytes 664
  3.2 0.0 copy-start.4
  3.2 0.7 %copy-done.4 = s32[160]{0:T(256)S(1)} copy-done((s32[160]{0:T(256)S(1)}, s32[160]{0:T(256)}, u32[]{:S(2)}) %copy-start.4) | copy-done | bytes 664
  3.8 0.0 copy-start.1
  3.8 0.0 copy-start.2
  3.9 0.0 copy-start.5
  3.9 0.0 copy-start.6
  3.9 0.0 copy-start.7
  3.9 0.0 copy-start.8
  3.9 4.9 %dense.1 = (bf16[1152,1024]{1,0:T(8,128)(2,1)S(1)}, bf16[1152,1024]{1,0:T(8,128)(2,1)S(1)}) custom-call(s32[160]{0:T(256)S(1)} %copy-done.3, s32[160]{0:T(256)S(1)} %copy-done.4, bf16[160,128,128]{2,1,0:T(8,128)(2,1)S(1)} %copy-done), custom_call_target="tpu_custom_call" | custom-call | tf_op jit(solution)/shard_map/dense/pallas_call | solution.py:62
  8.8 0.0 copy-done.1
  8.8 0.0 copy-done.2
  8.8 0.0 copy-done.5
  8.8 0.0 copy-done.6
  8.9 0.0 copy-done.7
  8.9 0.0 copy-done.8
  8.9 24.7 %spread.1 = f32[172,1024]{1,0:T(8,128)S(1)} custom-call(f32[2]{0:T(128)S(1)} %copy-done.5, s32[1,4]{1,0:T(1,128)S(1)} %copy-done.6, f32[172,1024]{1,0:T(8,128)S(1)} %copy-done.1, s32[1,4,32]{2,1,0:T(4,128)S(1)} %copy-done.2, s32[1,64]{1,0:T(1,128)S(1)} %bitcast.2, s32[1,64]{1,0:T(1,128)S(1)} %bitcast.3, bf16[1152,1024]{1,0:T(8,128)(2,1)S(1)} %get-tuple-element.7.high_in, ...), custom_call_target="tpu_custom_call" | custom-call | tf_op jit(solution)/shard_map/spread/pallas_call | solution.py:279
  33.6 0.9 %copy.11 = f32[172,1024]{1,0:T(8,128)} copy(f32[172,1024]{1,0:T(8,128)S(1)} %spread.1) | data formatting | bytes 1409024
Async XLA Ops:
  0.0 2.5 %copy-start = (bf16[160,128,128]{2,1,0:T(8,128)(2,1)S(1)}, bf16[160,128,128]{2,1,0:T(8,128)(2,1)}, u32[]{:S(2)}) copy-start(bf16[160,128,128]{2,1,0:T(8,128)(2,1)} %tiles.1) | copy-start | bytes 15728644
  2.5 0.7 %copy-start.3 = (s32[160]{0:T(256)S(1)}, s32[160]{0:T(256)}, u32[]{:S(2)}) copy-start(s32[160]{0:T(256)} %rows.1) | copy-start | bytes 1924
  3.2 0.7 %copy-start.4 = (s32[160]{0:T(256)S(1)}, s32[160]{0:T(256)}, u32[]{:S(2)}) copy-start(s32[160]{0:T(256)} %cols.1) | copy-start | bytes 1924
  3.8 5.0 %copy-start.1 = (f32[172,1024]{1,0:T(8,128)S(1)}, f32[172,1024]{1,0:T(8,128)}, u32[]{:S(2)}) copy-start(f32[172,1024]{1,0:T(8,128)} %base.1) | copy-start | bytes 2113540
  3.8 5.0 %copy-start.2 = (s32[1,4,32]{2,1,0:T(4,128)S(1)}, s32[1,4,32]{2,1,0:T(4,128)}, u32[]{:S(2)}) copy-start(s32[1,4,32]{2,1,0:T(4,128)} %send_rows.1) | copy-start | bytes 1540
  3.9 5.0 %copy-start.5 = (f32[2]{0:T(128)S(1)}, f32[2]{0:T(128)}, u32[]{:S(2)}) copy-start(f32[2]{0:T(128)} %alphas.1) | copy-start | bytes 28
  3.9 5.0 %copy-start.6 = (s32[1,4]{1,0:T(1,128)S(1)}, s32[1,4]{1,0:T(1,128)}, u32[]{:S(2)}) copy-start(s32[1,4]{1,0:T(1,128)} %counts.1) | copy-start | bytes 52
  3.9 5.0 %copy-start.7 = (s32[64]{0:T(128)S(1)}, s32[64]{0:T(128)}, u32[]{:S(2)}) copy-start(s32[64]{0:T(128)} %param.16) | copy-start | bytes 772
  3.9 5.0 %copy-start.8 = (s32[64]{0:T(128)S(1)}, s32[64]{0:T(128)}, u32[]{:S(2)}) copy-start(s32[64]{0:T(128)} %param.17) | copy-start | bytes 772
where the time goes:
time: 34.6 us; the launch traced here: 34.4 us
  Pallas kernels  29.6 us (86%)
  local copies, waits for them, and re-layouts  4.73 us (14%)
    pallas_call x1, Pallas kernels, shards(): pl.pallas_call(functools.partial(spread_body, n), out_shape=jax.ShapeDtyp...  24.7 us
    pallas_call x1, Pallas kernels, dense(): pl.pallas_call(dense_body, out_shape=(shape, shape), in_specs=[pl.BlockSp...  4.93 us
    unnamed x19, local copies, waits for them, and re-layouts  4.73 us

commit v1 on v0

v1 whole, which is shorter than its diff:
```python
import functools

import jax
import jax.numpy as jnp
from jax import lax
from jax.experimental import pallas as pl
from jax.experimental.pallas import tpu as pltpu
from jax.sharding import PartitionSpec as P

CHUNKS = 4
MESH = pl.DeviceIdType.MESH
BF = jnp.bfloat16
F32 = jnp.float32


def dot(a, b):
    return jnp.dot(a, b, preferred_element_type=F32)


def dot_nt(a, b, precision=None):
    return lax.dot_general(a, b, (((1,), (1,)), ((), ())), precision=precision, preferred_element_type=F32)


def dot_tn(a, b):
    return lax.dot_general(a, b, (((0,), (0,)), ((), ())), preferred_element_type=F32)


def split(x):
    high = x.astype(BF)
    return high, (x - high.astype(F32)).astype(BF)


def iota(shape, axis):
    return lax.broadcasted_iota(jnp.int32, shape, axis)


def ones_where(mask):
    return jnp.where(mask, 1.0, 0.0).astype(F32)


def bounded(index, size):
    return jnp.minimum(jnp.maximum(index, 0), size - 1)


def as_column(row):
    size = row.shape[1]
    eye = ones_where(iota((size, size), 0) == iota((size, size), 1))
    return dot_nt(eye, row, precision=lax.Precision.HIGHEST)


def tile_plan(rows, cols, row_blocks):
    count = rows.shape[1]
    key = (cols * row_blocks + rows).astype(F32)
    column = as_column(jnp.broadcast_to(key, (8, count)))[:, 0:1]
    square = (count, count)
    earlier = iota(square, 1) < iota(square, 0)
    twin = (key == column) & earlier
    rank = jnp.sum(ones_where((key < column) | twin), axis=1, keepdims=True)
    chained = jnp.sum(ones_where(twin), axis=1, keepdims=True) > 0.0
    placed = rank == iota(square, 1).astype(F32)
    order = jnp.sum(jnp.where(placed, iota(square, 0).astype(F32), 0.0), axis=0, keepdims=True)
    chain = jnp.sum(ones_where(placed & chained), axis=0, keepdims=True)
    block = iota(square, 1).astype(F32)
    upto = jnp.sum(ones_where(column <= block), axis=0, keepdims=True)
    any_tile = jnp.sum(ones_where(column == block), axis=0, keepdims=True) > 0.0
    last = jnp.where(any_tile, upto, 0.0)
    return order.astype(jnp.int32), chain.astype(jnp.int32), last.astype(jnp.int32)


def spread_body(
    n, alphas, counts, rows, cols, send_rows, nodes, labels, base_in, tiles, out,
    base, held, sums, high, low, pick, pick_high, pick_low, start, fixed, truth, plan, plan_s,
    sent0, sent1, sent2, sent3, sent4, got0, got1, got2, got3, got4,
    part, parts, send_sems, recv_sems, part_send, part_recv, load_sems,
):
    channels, local = base.shape
    count, tile, _ = held.shape
    row_blocks, col_blocks = local // tile, high.shape[0] // tile
    slots, size = send_rows.shape[1:]
    halo = slots * size
    reach = slots // 2
    offsets = [value for value in range(-reach, reach + 1) if value != 0]
    me = lax.axis_index("row")
    sent, got = (sent0, sent1, sent2, sent3, sent4), (got0, got1, got2, got3, got4)

    barrier = pltpu.get_barrier_semaphore()

    def greet(k, _):
        pl.semaphore_signal(barrier, inc=1, device_id={"row": lax.rem(me + k, n)}, device_id_type=MESH)
        return 0

    lax.fori_loop(1, n, greet, 0)
    base_load = pltpu.make_async_copy(base_in, base, load_sems.at[0])
    base_load.start()
    step = count // CHUNKS
    loads = []
    for chunk in range(CHUNKS):
        some = pl.ds(chunk * step, step)
        loads.append(pltpu.make_async_copy(tiles.at[some], held.at[some], load_sems.at[2 + chunk]))
        loads[-1].start()

    def inside(offset):
        return (me + offset >= 0) & (me + offset < n)

    for slot, offset in enumerate(offsets):

        @pl.when(jnp.logical_not(inside(offset)))
        def _():
            for buffer in got:
                buffer[slot] = jnp.zeros(buffer.shape[1:], buffer.dtype)

    def copy(turn, k):
        return pltpu.make_async_remote_copy(
            src_ref=sent[turn].at[k],
            dst_ref=got[turn].at[slots - 1 - k],
            send_sem=send_sems.at[turn, k],
            recv_sem=recv_sems.at[turn, slots - 1 - k],
            device_id={"row": me + offsets[k]},
            device_id_type=MESH,
        )

    def send(turn, picked):
        for k in range(slots):
            sent[turn][k] = picked[k * size : (k + 1) * size, :].astype(sent[turn].dtype)
        for k, offset in enumerate(offsets):

            @pl.when(inside(offset))
            def _():
                copy(turn, k).start()

    def receive(turn):
        for slot, offset in enumerate(offsets):

            @pl.when(inside(offset))
            def _():
                copy(turn, slots - 1 - slot).wait_recv()

        return jnp.concatenate([got[turn][slot] for slot in range(slots)], axis=0)

    def local_product(values):
        return dot(values, high[:local, :]) + dot(values, low[:local, :])

    def halo_product(values):
        return dot_tn(values, high[local:, :]) + dot_tn(values, low[local:, :])

    def picked_local(values):
        return dot_nt(pick_high[:, :local], values) + dot_nt(pick_low[:, :local], values)

    def picked_halo(values):
        return dot(pick_high[:, local:], values) + dot(pick_low[:, local:], values)

    wanted = as_column(send_rows[0].astype(F32)).astype(jnp.int32)
    column, place = iota((size, local), 1), iota((size, local), 0)
    for k in range(slots):
        live = (column == wanted[:, k : k + 1]) & (place < counts[0, k])
        pick[k * size : (k + 1) * size, :] = ones_where(live).astype(BF)
    labelled_count = nodes.shape[1]
    node = as_column(jnp.broadcast_to(nodes[...].astype(F32), (8, labelled_count)))[:, 0:1].astype(jnp.int32)
    placed = ones_where(iota((labelled_count, local), 1) == node).astype(BF)
    pick[halo:, :] = placed
    onehot = ones_where(iota((channels, labelled_count), 0) == labels[...]).astype(BF)
    truth[...] = dot(onehot, placed)
    labelled = dot(jnp.ones((8, labelled_count), BF), placed)
    free = 1.0 - labelled[0:1, :]
    base_load.wait()
    start[...] = labelled[0:1, :] * (truth[...] - base[...])
    values = start[...].astype(BF)
    first = dot_nt(pick[:halo, :], values)
    pl.semaphore_wait(barrier, n - 1)
    send(0, first)

    order, chain, last = tile_plan(rows[...], cols[...], row_blocks)
    plan[...] = jnp.zeros_like(plan)
    plan[0:1, :count] = order
    plan[1:2, :count] = chain
    plan[2:3, :count] = last
    plan_copy = pltpu.make_async_copy(plan, plan_s, load_sems.at[1])
    plan_copy.start()

    fixed[...] = truth[...] + free * base[...]
    rest = base[...]
    base_pick = jnp.zeros((pick.shape[0], channels), F32)
    for _ in range(3):
        term = rest.astype(BF)
        rest = rest - term.astype(F32)
        base_pick = base_pick + dot_nt(pick[...], term)
    truth_pick = dot_nt(pick[...], truth[...].astype(BF))
    labelled_pick = dot_nt(pick[...], labelled.astype(BF))[:, 0:1]
    live_pick = dot_nt(pick[...], jnp.ones((8, local), BF))[:, 0:1]
    free_pick = live_pick - labelled_pick
    start_pick = labelled_pick * (truth_pick - base_pick)
    fixed_pick = truth_pick + free_pick * base_pick

    sums[0] = jnp.zeros((tile, tile), F32)
    plan_copy.wait()
    for load in loads:
        load.wait()

    def add(k, running):
        keep = jnp.full((tile, tile), plan_s[1, k], jnp.int32) > 0
        running = jnp.where(keep, running, 0.0) + held[bounded(plan_s[0, k], count)].astype(F32)
        sums[k + 1] = running
        return running

    lax.fori_loop(0, count, add, jnp.zeros((tile, tile), F32))

    def settle(c, _):
        for r in range(row_blocks):
            high_part, low_part = split(sums[bounded(plan_s[2, c * row_blocks + r], count + 1)])
            where = (pl.ds(pl.multiple_of(c * tile, tile), tile), pl.ds(r * tile, tile))
            high[where] = high_part
            low[where] = low_part
        return 0

    lax.fori_loop(0, col_blocks, settle, 0)
    pick_high[...] = dot_nt(pick[...], high[...]).astype(BF)
    pick_low[...] = dot_nt(pick[...], low[...]).astype(BF)

    def folded(x):
        row = jnp.sum(x, axis=0, keepdims=True)
        return jnp.broadcast_to(jnp.sum(row, axis=1, keepdims=True), (1, 128))

    weight = alphas[0]
    picked = picked_local(values)
    total = local_product(values)
    edge = receive(0)
    picked = picked + picked_halo(edge)
    picked = (1.0 - weight) * start_pick + weight * picked
    send(1, picked)
    send(4, fixed_pick)
    total = total + halo_product(edge)
    values = ((1.0 - weight) * start[...] + weight * total).astype(BF)

    picked = picked_local(values)
    total = local_product(values)
    edge = receive(1)
    picked = picked + picked_halo(edge)
    picked = (1.0 - weight) * start_pick + weight * picked
    part[...] = jnp.zeros_like(part)
    part[0:1, :] = folded(jnp.abs(start_pick[halo:, :]))
    part[1:2, :] = folded(jnp.abs(picked[halo:, :]))

    def part_copy(k):
        return pltpu.make_async_remote_copy(
            src_ref=part,
            dst_ref=parts.at[k - 1],
            send_sem=part_send.at[k - 1],
            recv_sem=part_recv.at[k - 1],
            device_id={"row": lax.rem(me + k, n)},
            device_id_type=MESH,
        )

    def part_start(k, _):
        part_copy(k).start()
        return 0

    lax.fori_loop(1, n, part_start, 0)
    moving_pick = free_pick * picked
    send(2, moving_pick)
    total = total + halo_product(edge)
    moving = free * ((1.0 - weight) * start[...] + weight * total)

    def part_wait(k, _):
        part_copy(k).wait_recv()
        return 0

    lax.fori_loop(1, n, part_wait, 0)
    sums_all = part[...] + jnp.sum(parts[...], axis=0)
    entries = n * labelled_count * channels
    scale = (sums_all[0:1, 0:1] / entries) / (sums_all[1:2, 0:1] / entries + 1e-06)
    start[...] = fixed[...] + scale * moving
    anchored_pick = fixed_pick + scale * moving_pick

    weight = alphas[1]
    values = start[...].astype(BF)
    picked = picked_local(values)
    fixed_edge = receive(4)
    edge = (fixed_edge + scale * receive(2)).astype(BF)
    picked = picked + picked_halo(edge)
    send(3, truth_pick + free_pick * ((1.0 - weight) * anchored_pick + weight * picked))
    total = local_product(values) + halo_product(edge)
    values = (truth[...] + free * ((1.0 - weight) * start[...] + weight * total)).astype(BF)

    total = local_product(values)
    total = total + halo_product(receive(3))
    out[...] = truth[...] + free * ((1.0 - weight) * start[...] + weight * total)

    for turn in range(len(sent)):
        for k, offset in enumerate(offsets):

            @pl.when(inside(offset))
            def _():
                copy(turn, k).wait_send()

    def part_end(k, _):
        part_copy(k).wait_send()
        return 0

    lax.fori_loop(1, n, part_end, 0)


def shards(
    alphas, base_scores, tile_values, tile_rows, tile_cols, send_rows, send_count, train_nodes, train_labels
):
    n = lax.axis_size("row")
    channels, local = base_scores.shape
    slots, size = send_rows.shape[1:]
    count, tile, _ = tile_values.shape
    halo = slots * size
    picks = halo + train_nodes.shape[0]
    vmem = pl.BlockSpec(memory_space=pltpu.VMEM)
    smem = pl.BlockSpec(memory_space=pltpu.SMEM)
    hbm = pl.BlockSpec(memory_space=pl.ANY)
    whole = pltpu.VMEM((channels, local), F32)
    lanes = -(-count // 128) * 128
    boundary = [pltpu.VMEM((slots, size, channels), kind) for kind in (BF, BF, F32, BF, F32)]
    return pl.pallas_call(
        functools.partial(spread_body, n),
        out_shape=jax.ShapeDtypeStruct((channels, local), F32),
        in_specs=[smem, smem, vmem, vmem, vmem, vmem, vmem, hbm, hbm],
        out_specs=vmem,
        scratch_shapes=[
            whole,
            pltpu.VMEM(tile_values.shape, BF),
            pltpu.VMEM((count + 1, tile, tile), F32),
            pltpu.VMEM((local + halo, local), BF),
            pltpu.VMEM((local + halo, local), BF),
            pltpu.VMEM((picks, local), BF),
            pltpu.VMEM((picks, local + halo), BF),
            pltpu.VMEM((picks, local + halo), BF),
            whole,
            whole,
            whole,
            pltpu.VMEM((8, lanes), jnp.int32),
            pltpu.SMEM((8, lanes), jnp.int32),
            *boundary,
            *boundary,
            pltpu.VMEM((8, 128), F32),
            pltpu.VMEM((n - 1, 8, 128), F32),
            pltpu.SemaphoreType.DMA((5, slots)),
            pltpu.SemaphoreType.DMA((5, slots)),
            pltpu.SemaphoreType.DMA((n - 1,)),
            pltpu.SemaphoreType.DMA((n - 1,)),
            pltpu.SemaphoreType.DMA((2 + CHUNKS,)),
        ],
        compiler_params=pltpu.CompilerParams(collective_id=0, has_side_effects=True, vmem_limit_bytes=60 << 20),
        name="spread",
    )(
        alphas, send_count, tile_rows.reshape(1, -1), tile_cols.reshape(1, -1), send_rows,
        train_nodes.reshape(1, -1), train_labels.reshape(1, -1), base_scores, tile_values,
    )


def solution(mesh):
    return jax.shard_map(
        shards,
        mesh=mesh,
        in_specs=(
            P("sweep"), P(None, "row"), P("row", None, None), P("row"), P("row"),
            P("row", None, None), P("row", None), P("row"), P("row"),
        ),
        out_specs=P("sweep", "row"),
        check_vma=False,
    )
```

time: 34.6 us -> 30.4 us (0.88)
  local copies, waits for them, and re-layouts: 4.73 us -> 2.04 us
  Pallas kernels: 29.6 us -> 28.2 us
    pallas_call x1 -> x0, Pallas kernels: 4.93 us -> none  [dense(): pl.pallas_call(dense_body, out_shape=(shape, shape), in_specs=[pl.BlockSp...]
    pallas_call x1, Pallas kernels: 24.7 us -> 28.2 us  [shards(): pl.pallas_call(functools.partial(spread_body, n), out_shape=jax.ShapeDtyp...]
    unnamed x19 -> x1, local copies, waits for them, and re-layouts: 4.73 us -> 2.04 us
where the time goes in v1:
time: 30.4 us; the launch traced here: 30.3 us
  Pallas kernels  28.2 us (93%)
  local copies, waits for them, and re-layouts  2.04 us (7%)
    pallas_call x1, Pallas kernels, shards(): pl.pallas_call(functools.partial(spread_body, n), out_shape=jax.ShapeDtyp...  28.2 us
    unnamed x1, local copies, waits for them, and re-layouts  2.04 us

profile of v1, /device:TPU:0, one launch (start us, length us, event | category | flops | bytes accessed | tf_op | source)
XLA Modules:
  0.0 30.3 jit_solution(10800308807975909565)
XLA Ops:
  0.0 28.2 %spread.1 = f32[172,1024]{1,0:T(8,128)} custom-call(f32[2]{0:T(128)} %alphas.1, s32[1,4]{1,0:T(1,128)} %counts.1, s32[1,160]{1,0:T(1,128)} %bitcast.4, s32[1,160]{1,0:T(1,128)} %bitcast.5, s32[1,4,32]{2,1,0:T(4,128)} %send_rows.1, s32[1,64]{1,0:T(1,128)} %bitcast.6, s32[1,64]{1,0:T(1,128)} %bitcast.7, f32[172,1024]{1,0:T(8,128)} %base_in.1, ...), custom_call_target="tpu_custom_call" | custom-call | tf_op jit(solution)/shard_map/spread/pallas_call | solution.py:317
  28.2 2.0 %copy.11 = f32[172,1024]{1,0:T(8,128)} copy(f32[172,1024]{1,0:T(8,128)} %spread.1) | data formatting | bytes 1409024

commit v2 on v1

--- a/solution.py
+++ b/solution.py
@@ -8,6 +8,8 @@
 from jax.sharding import PartitionSpec as P
 
 CHUNKS = 4
+WIDTH = 256
+LIMIT = 56 << 20
 MESH = pl.DeviceIdType.MESH
 BF = jnp.bfloat16
 F32 = jnp.float32
@@ -69,7 +71,7 @@
 
 def spread_body(
     n, alphas, counts, rows, cols, send_rows, nodes, labels, base_in, tiles, out,
-    base, held, sums, high, low, pick, pick_high, pick_low, start, fixed, truth, plan, plan_s,
+    base, held, sums, high, low, pick, pick_high, pick_low, start, fixed, truth, free, wide0, wide1, total, plan, plan_s,
     sent0, sent1, sent2, sent3, sent4, got0, got1, got2, got3, got4,
     part, parts, send_sems, recv_sems, part_send, part_recv, load_sems,
 ):
@@ -137,17 +139,29 @@
 
         return jnp.concatenate([got[turn][slot] for slot in range(slots)], axis=0)
 
-    def local_product(values):
-        return dot(values, high[:local, :]) + dot(values, low[:local, :])
-
-    def halo_product(values):
-        return dot_tn(values, high[local:, :]) + dot_tn(values, low[local:, :])
+    def over_columns(step):
+        def one(j, _):
+            step(pl.ds(pl.multiple_of(j * WIDTH, WIDTH), WIDTH))
+            return 0
+
+        lax.fori_loop(0, local // WIDTH, one, 0)
+
+    def product(values, rows, columns):
+        return dot(values, high[rows, columns]) + dot(values, low[rows, columns])
 
     def picked_local(values):
         return dot_nt(pick_high[:, :local], values) + dot_nt(pick_low[:, :local], values)
 
     def picked_halo(values):
         return dot(pick_high[:, local:], values) + dot(pick_low[:, local:], values)
+
+    order, chain, last = tile_plan(rows[...], cols[...], row_blocks)
+    plan[...] = jnp.zeros_like(plan)
+    plan[0:1, :count] = order
+    plan[1:2, :count] = chain
+    plan[2:3, :count] = last
+    plan_copy = pltpu.make_async_copy(plan, plan_s, load_sems.at[1])
+    plan_copy.start()
 
     wanted = as_column(send_rows[0].astype(F32)).astype(jnp.int32)
     column, place = iota((size, local), 1), iota((size, local), 0)
@@ -161,23 +175,15 @@
     onehot = ones_where(iota((channels, labelled_count), 0) == labels[...]).astype(BF)
     truth[...] = dot(onehot, placed)
     labelled = dot(jnp.ones((8, labelled_count), BF), placed)
-    free = 1.0 - labelled[0:1, :]
+    free[...] = 1.0 - labelled
     base_load.wait()
     start[...] = labelled[0:1, :] * (truth[...] - base[...])
-    values = start[...].astype(BF)
-    first = dot_nt(pick[:halo, :], values)
+    wide0[:, :local] = start[...].astype(BF)
+    first = dot_nt(pick[:halo, :], wide0[:, :local])
     pl.semaphore_wait(barrier, n - 1)
     send(0, first)
 
-    order, chain, last = tile_plan(rows[...], cols[...], row_blocks)
-    plan[...] = jnp.zeros_like(plan)
-    plan[0:1, :count] = order
-    plan[1:2, :count] = chain
-    plan[2:3, :count] = last
-    plan_copy = pltpu.make_async_copy(plan, plan_s, load_sems.at[1])
-    plan_copy.start()
-
-    fixed[...] = truth[...] + free * base[...]
+    fixed[...] = truth[...] + free[0:1, :] * base[...]
     rest = base[...]
     base_pick = jnp.zeros((pick.shape[0], channels), F32)
     for _ in range(3):
@@ -202,7 +208,7 @@
         sums[k + 1] = running
         return running
 
-    lax.fori_loop(0, count, add, jnp.zeros((tile, tile), F32))
+    lax.fori_loop(0, count, add, jnp.zeros((tile, tile), F32), unroll=8)
 
     def settle(c, _):
         for r in range(row_blocks):
@@ -213,26 +219,36 @@
         return 0
 
     lax.fori_loop(0, col_blocks, settle, 0)
-    pick_high[...] = dot_nt(pick[...], high[...]).astype(BF)
-    pick_low[...] = dot_nt(pick[...], low[...]).astype(BF)
+    group = (local + halo) // 3
+
+    def pick_columns(j, _):
+        columns = pl.ds(pl.multiple_of(j * group, tile), group)
+        pick_high[:, columns] = dot_nt(pick[...], high[columns, :]).astype(BF)
+        pick_low[:, columns] = dot_nt(pick[...], low[columns, :]).astype(BF)
+        return 0
+
+    lax.fori_loop(0, 3, pick_columns, 0)
 
     def folded(x):
         row = jnp.sum(x, axis=0, keepdims=True)
         return jnp.broadcast_to(jnp.sum(row, axis=1, keepdims=True), (1, 128))
 
     weight = alphas[0]
-    picked = picked_local(values)
-    total = local_product(values)
+    picked = picked_local(wide0[:, :local])
     edge = receive(0)
     picked = picked + picked_halo(edge)
     picked = (1.0 - weight) * start_pick + weight * picked
     send(1, picked)
     send(4, fixed_pick)
-    total = total + halo_product(edge)
-    values = ((1.0 - weight) * start[...] + weight * total).astype(BF)
-
-    picked = picked_local(values)
-    total = local_product(values)
+    wide0[:, local:] = edge.T
+
+    def first_hop(columns):
+        spread = product(wide0[...], slice(None), columns)
+        wide1[:, columns] = ((1.0 - weight) * start[:, columns] + weight * spread).astype(BF)
+
+    over_columns(first_hop)
+
+    picked = picked_local(wide1[:, :local])
     edge = receive(1)
     picked = picked + picked_halo(edge)
     picked = (1.0 - weight) * start_pick + weight * picked
@@ -257,8 +273,13 @@
     lax.fori_loop(1, n, part_start, 0)
     moving_pick = free_pick * picked
     send(2, moving_pick)
-    total = total + halo_product(edge)
-    moving = free * ((1.0 - weight) * start[...] + weight * total)
+    wide1[:, local:] = edge.T
+
+    def second_hop(columns):
+        spread = product(wide1[...], slice(None), columns)
+        total[:, columns] = free[0:1, columns] * ((1.0 - weight) * start[:, columns] + weight * spread)
+
+    over_columns(second_hop)
 
     def part_wait(k, _):
         part_copy(k).wait_recv()
@@ -268,22 +289,37 @@
     sums_all = part[...] + jnp.sum(parts[...], axis=0)
     entries = n * labelled_count * channels
     scale = (sums_all[0:1, 0:1] / entries) / (sums_all[1:2, 0:1] / entries + 1e-06)
-    start[...] = fixed[...] + scale * moving
+    start[...] = fixed[...] + scale * total[...]
+    wide0[:, :local] = start[...].astype(BF)
     anchored_pick = fixed_pick + scale * moving_pick
 
     weight = alphas[1]
-    values = start[...].astype(BF)
-    picked = picked_local(values)
+    picked = picked_local(wide0[:, :local])
     fixed_edge = receive(4)
     edge = (fixed_edge + scale * receive(2)).astype(BF)
     picked = picked + picked_halo(edge)
     send(3, truth_pick + free_pick * ((1.0 - weight) * anchored_pick + weight * picked))
-    total = local_product(values) + halo_product(edge)
-    values = (truth[...] + free * ((1.0 - weight) * start[...] + weight * total)).astype(BF)
-
-    total = local_product(values)
-    total = total + halo_product(receive(3))
-    out[...] = truth[...] + free * ((1.0 - weight) * start[...] + weight * total)
+    wide0[:, local:] = edge.T
+
+    def third_hop(columns):
+        spread = product(wide0[...], slice(None), columns)
+        smoothed = (1.0 - weight) * start[:, columns] + weight * spread
+        wide1[:, columns] = (truth[:, columns] + free[0:1, columns] * smoothed).astype(BF)
+
+    over_columns(third_hop)
+
+    def fourth_hop(columns):
+        total[:, columns] = product(wide1[:, :local], slice(0, local), columns)
+
+    over_columns(fourth_hop)
+    wide1[:, local:] = receive(3).T
+
+    def finish(columns):
+        spread = total[:, columns] + product(wide1[:, local:], slice(local, None), columns)
+        smoothed = (1.0 - weight) * start[:, columns] + weight * spread
+        out[:, columns] = truth[:, columns] + free[0:1, columns] * smoothed
+
+    over_columns(finish)
 
     for turn in range(len(sent)):
         for k, offset in enumerate(offsets):
@@ -312,11 +348,12 @@
     smem = pl.BlockSpec(memory_space=pltpu.SMEM)
     hbm = pl.BlockSpec(memory_space=pl.ANY)
     whole = pltpu.VMEM((channels, local), F32)
+    wide = pltpu.VMEM((channels, local + halo), BF)
     lanes = -(-count // 128) * 128
     boundary = [pltpu.VMEM((slots, size, channels), kind) for kind in (BF, BF, F32, BF, F32)]
     return pl.pallas_call(
         functools.partial(spread_body, n),
-        out_shape=jax.ShapeDtypeStruct((channels, local), F32),
+        out_shape=pltpu.VMEM((channels, local), F32),
         in_specs=[smem, smem, vmem, vmem, vmem, vmem, vmem, hbm, hbm],
         out_specs=vmem,
         scratch_shapes=[
@@ -331,6 +368,10 @@
             whole,
             whole,
             whole,
+            pltpu.VMEM((8, local), F32),
+            wide,
+            wide,
+            whole,
             pltpu.VMEM((8, lanes), jnp.int32),
             pltpu.SMEM((8, lanes), jnp.int32),
             *boundary,
@@ -343,7 +384,7 @@
             pltpu.SemaphoreType.DMA((n - 1,)),
             pltpu.SemaphoreType.DMA((2 + CHUNKS,)),
         ],
-        compiler_params=pltpu.CompilerParams(collective_id=0, has_side_effects=True, vmem_limit_bytes=60 << 20),
+        compiler_params=pltpu.CompilerParams(collective_id=0, has_side_effects=True, vmem_limit_bytes=LIMIT),
         name="spread",
     )(
         alphas, send_count, tile_rows.reshape(1, -1), tile_cols.reshape(1, -1), send_rows,

time: 30.4 us -> 27 us (0.89)
  Pallas kernels: 28.2 us -> 26 us
  local copies, waits for them, and re-layouts: 2.04 us -> 0.86 us
    pallas_call x1, Pallas kernels: 28.2 us -> 26 us  [shards(): pl.pallas_call(functools.partial(spread_body, n), out_shape=pltpu.VMEM((c...]
    unnamed x1, local copies, waits for them, and re-layouts: 2.04 us -> 0.86 us
where the time goes in v2:
time: 27 us; the launch traced here: 26.9 us
  Pallas kernels  26 us (96%)
  local copies, waits for them, and re-layouts  0.86 us (3%)
    pallas_call x1, Pallas kernels, shards(): pl.pallas_call(functools.partial(spread_body, n), out_shape=pltpu.VMEM((c...  26 us
    unnamed x1, local copies, waits for them, and re-layouts  0.86 us

profile of v2, /device:TPU:0, one launch (start us, length us, event | category | flops | bytes accessed | tf_op | source)
XLA Modules:
  0.0 26.9 jit_solution(5779951043233775020)
XLA Ops:
  0.0 26.0 %spread.1 = f32[172,1024]{1,0:T(8,128)S(1)} custom-call(f32[2]{0:T(128)} %alphas.1, s32[1,4]{1,0:T(1,128)} %counts.1, s32[1,160]{1,0:T(1,128)} %bitcast.4, s32[1,160]{1,0:T(1,128)} %bitcast.5, s32[1,4,32]{2,1,0:T(4,128)} %send_rows.1, s32[1,64]{1,0:T(1,128)} %bitcast.6, s32[1,64]{1,0:T(1,128)} %bitcast.7, f32[172,1024]{1,0:T(8,128)} %base_in.1, ...), custom_call_target="tpu_custom_call" | custom-call | tf_op jit(solution)/shard_map/spread/pallas_call | solution.py:354
  26.0 0.9 %copy.11 = f32[172,1024]{1,0:T(8,128)} copy(f32[172,1024]{1,0:T(8,128)S(1)} %spread.1) | data formatting | bytes 1409024

commit v3 on v2

--- a/solution.py
+++ b/solution.py
@@ -231,7 +231,7 @@
 
     def folded(x):
         row = jnp.sum(x, axis=0, keepdims=True)
-        return jnp.broadcast_to(jnp.sum(row, axis=1, keepdims=True), (1, 128))
+        return jnp.sum(row, axis=1, keepdims=True)
 
     weight = alphas[0]
     picked = picked_local(wide0[:, :local])
@@ -252,9 +252,8 @@
     edge = receive(1)
     picked = picked + picked_halo(edge)
     picked = (1.0 - weight) * start_pick + weight * picked
-    part[...] = jnp.zeros_like(part)
-    part[0:1, :] = folded(jnp.abs(start_pick[halo:, :]))
-    part[1:2, :] = folded(jnp.abs(picked[halo:, :]))
+    mass, spread_mass = folded(jnp.abs(start_pick[halo:, :])), folded(jnp.abs(picked[halo:, :]))
+    part[...] = jnp.where(iota((1, 128), 1) < 64, mass, spread_mass)
 
     def part_copy(k):
         return pltpu.make_async_remote_copy(
@@ -288,7 +287,7 @@
     lax.fori_loop(1, n, part_wait, 0)
     sums_all = part[...] + jnp.sum(parts[...], axis=0)
     entries = n * labelled_count * channels
-    scale = (sums_all[0:1, 0:1] / entries) / (sums_all[1:2, 0:1] / entries + 1e-06)
+    scale = (sums_all[:, 0:1] / entries) / (sums_all[:, 64:65] / entries + 1e-06)
     start[...] = fixed[...] + scale * total[...]
     wide0[:, :local] = start[...].astype(BF)
     anchored_pick = fixed_pick + scale * moving_pick
@@ -376,8 +375,8 @@
             pltpu.SMEM((8, lanes), jnp.int32),
             *boundary,
             *boundary,
-            pltpu.VMEM((8, 128), F32),
-            pltpu.VMEM((n - 1, 8, 128), F32),
+            pltpu.VMEM((1, 128), F32),
+            pltpu.VMEM((n - 1, 1, 128), F32),
             pltpu.SemaphoreType.DMA((5, slots)),
             pltpu.SemaphoreType.DMA((5, slots)),
             pltpu.SemaphoreType.DMA((n - 1,)),

time: 27 us -> 26.9 us (level)
  no operation moved by 1% of the time
where the time goes in v3:
time: 26.9 us; the launch traced here: 26.7 us
  Pallas kernels  25.9 us (96%)
  local copies, waits for them, and re-layouts  0.86 us (3%)
    pallas_call x1, Pallas kernels, shards(): pl.pallas_call(functools.partial(spread_body, n), out_shape=pltpu.VMEM((c...  25.9 us
    unnamed x1, local copies, waits for them, and re-layouts  0.86 us

profile of v3, /device:TPU:0, one launch (start us, length us, event | category | flops | bytes accessed | tf_op | source)
XLA Modules:
  0.0 26.7 jit_solution(1728930210174817802)
XLA Ops:
  0.0 25.9 %spread.1 = f32[172,1024]{1,0:T(8,128)S(1)} custom-call(f32[2]{0:T(128)} %alphas.1, s32[1,4]{1,0:T(1,128)} %counts.1, s32[1,160]{1,0:T(1,128)} %bitcast.4, s32[1,160]{1,0:T(1,128)} %bitcast.5, s32[1,4,32]{2,1,0:T(4,128)} %send_rows.1, s32[1,64]{1,0:T(1,128)} %bitcast.6, s32[1,64]{1,0:T(1,128)} %bitcast.7, f32[172,1024]{1,0:T(8,128)} %base_in.1, ...), custom_call_target="tpu_custom_call" | custom-call | tf_op jit(solution)/shard_map/spread/pallas_call | solution.py:353
  25.9 0.9 %copy.11 = f32[172,1024]{1,0:T(8,128)} copy(f32[172,1024]{1,0:T(8,128)S(1)} %spread.1) | data formatting | bytes 1409024

commit v4 on v3

--- a/solution.py
+++ b/solution.py
@@ -8,7 +8,7 @@
 from jax.sharding import PartitionSpec as P
 
 CHUNKS = 4
-WIDTH = 256
+WIDTH = 1024
 LIMIT = 56 << 20
 MESH = pl.DeviceIdType.MESH
 BF = jnp.bfloat16

time: 26.9 us -> 26.5 us (0.985)
  Pallas kernels: 25.9 us -> 25.5 us
    pallas_call x1, Pallas kernels: 25.9 us -> 25.5 us  [shards(): pl.pallas_call(functools.partial(spread_body, n), out_shape=pltpu.VMEM((c...]
where the time goes in v4:
time: 26.5 us; the launch traced here: 26.4 us
  Pallas kernels  25.5 us (96%)
  local copies, waits for them, and re-layouts  0.86 us (3%)
    pallas_call x1, Pallas kernels, shards(): pl.pallas_call(functools.partial(spread_body, n), out_shape=pltpu.VMEM((c...  25.5 us
    unnamed x1, local copies, waits for them, and re-layouts  0.86 us

profile of v4, /device:TPU:0, one launch (start us, length us, event | category | flops | bytes accessed | tf_op | source)
XLA Modules:
  0.0 26.4 jit_solution(5735385741561237268)
XLA Ops:
  0.0 25.5 %spread.1 = f32[172,1024]{1,0:T(8,128)S(1)} custom-call(f32[2]{0:T(128)} %alphas.1, s32[1,4]{1,0:T(1,128)} %counts.1, s32[1,160]{1,0:T(1,128)} %bitcast.4, s32[1,160]{1,0:T(1,128)} %bitcast.5, s32[1,4,32]{2,1,0:T(4,128)} %send_rows.1, s32[1,64]{1,0:T(1,128)} %bitcast.6, s32[1,64]{1,0:T(1,128)} %bitcast.7, f32[172,1024]{1,0:T(8,128)} %base_in.1, ...), custom_call_target="tpu_custom_call" | custom-call | tf_op jit(solution)/shard_map/spread/pallas_call | solution.py:353
  25.5 0.9 %copy.11 = f32[172,1024]{1,0:T(8,128)} copy(f32[172,1024]{1,0:T(8,128)S(1)} %spread.1) | data formatting | bytes 1409024
